TPU v7x, 32 devices: a whole 2x2x4 slice. The times are simulated.
32 devices in a mesh: dp: 4 (over z), seq: 8 (over y, x, core).
Axes of the slice: x: 2, y: 2, z: 4, core: 2. Of those that a mesh axis runs over, the one named last changes fastest.
Arguments:
- tokens: bfloat16 [4096, 8192], P(('dp', 'seq')), may hold values from -6 to 6
- queries: bfloat16 [4096, 1024], P(('dp', 'seq')), may hold values from -110 to 110
- positions: int32 [4096], P(('dp', 'seq')), may hold values from 0 to 255, as said below
- grad: float32 [8192, 256], P(('dp', 'seq')), may hold values from -6 to 6
- master: float32 [8192, 256], P(('dp', 'seq')), may hold values from -0.0625 to 0.0625
- moment1: float32 [8192, 256], P(('dp', 'seq')), may hold values from -1.8 to 1.8
- moment2: float32 [8192, 256], P(('dp', 'seq')), may hold values from 0.5 to 4
- step: int32 [1], replicated, may hold values from 1 to 8
Outputs:
- attention: bfloat16 [4096, 1024], P(('dp', 'seq'))
- new_master: float32 [8192, 256], P(('dp', 'seq'))
- new_first: float32 [8192, 256], P(('dp', 'seq'))
- new_second: float32 [8192, 256], P(('dp', 'seq'))
Inputs may be any that keep to these rules, and one draw needn't show every extreme that they name: `positions`: the sequence is a pack of documents of 1 to 256 tokens, one of exactly 256; a position is 0 at the first token of each document and rises by one from token to token inside a document.
All inputs are finite; a program needn't handle non-finite values.
Results may differ from a plain program's by a relative error of at most 0.014.
The roundings to bfloat16 on the way count: a program that leaves them out, or rounds other values in their place, can miss the bound.
Values may be sent and summed in bfloat16 or wider, within the bound.
A program may use at most 64 MiB of HBM per device.

v0:
```python
import math

import jax
import jax.numpy as jnp
from jax import lax
from jax.sharding import PartitionSpec as P

GROUP = 8


beta_one = 0.9
beta_two = 0.95
learn_rate = 0.02
adam_eps = 1e-08
rope_base = 500000.0
masked_score = -1e30


def shifted(value, axis, steps):
    count = lax.axis_size(axis)
    first, last = (max(0, -steps), min(count, count - steps))
    return lax.ppermute(value, axis, [(source, source + steps) for source in range(first, last)])


def rotate_pairs(values_in, places):
    half_width = values_in.shape[-1] // 2
    freqs = jnp.exp(
        jnp.arange(half_width, dtype=jnp.float32)
        * (-2.0 * math.log(rope_base) / values_in.shape[-1])
    )
    angles = places.astype(jnp.float32)[:, None, None] * freqs
    cosine = jnp.cos(angles)
    sine = jnp.sin(angles)
    first = values_in[..., :half_width]
    second = values_in[..., half_width:]
    return jnp.concatenate(
        [first * cosine - second * sine, second * cosine + first * sine], axis=-1
    )


def adam_update(grad, master, moment1, moment2, step):
    counter = step[0].astype(jnp.float32)
    new_first = beta_one * moment1 + (1.0 - beta_one) * grad
    new_second = beta_two * moment2 + (1.0 - beta_two) * grad * grad
    fixed_first = new_first / (1.0 - jnp.power(jnp.float32(beta_one), counter))
    fixed_second = new_second / (1.0 - jnp.power(jnp.float32(beta_two), counter))
    new_master = master - learn_rate * fixed_first / (jnp.sqrt(fixed_second) + adam_eps)
    return (new_master, new_first, new_second)


def attend_rows(query_rows, query_global, query_places, keys, values_v, key_global):
    row_count = query_rows.shape[0]
    block = 512

    def one_block(triple):
        rows, index, places = triple
        scores = jnp.einsum(
            "rd,kd->rk", rows, keys, preferred_element_type=jnp.float32
        ) * rows.shape[-1] ** (-0.5)
        allowed = (key_global[None, :] <= index[:, None]) & (
            key_global[None, :] >= (index - places)[:, None]
        )
        scores = jnp.where(allowed, scores, masked_score)
        top_score = jnp.max(scores, axis=1, keepdims=True)
        weights = jnp.exp(scores - top_score)
        totals = jnp.sum(weights, axis=1, keepdims=True)
        probs = (weights / totals).astype(jnp.bfloat16)
        return jnp.dot(probs, values_v, preferred_element_type=jnp.float32).astype(jnp.bfloat16)

    blocks = lax.map(
        one_block,
        (
            query_rows.reshape(-1, block, query_rows.shape[1]),
            query_global.reshape(-1, block),
            query_places.reshape(-1, block),
        ),
    )
    return blocks.reshape(row_count, -1)


def local(tokens, queries, positions, grad, master, moment1, moment2, step):
    new_master, new_first, new_second = adam_update(grad, master, moment1, moment2, step)
    weight = new_master.astype(jnp.bfloat16)
    head_dim = weight.shape[1] // 2
    local_count = tokens.shape[0]
    projected = jnp.dot(
        tokens,
        lax.all_gather(weight, ("dp", "seq"), axis=0, tiled=True),
        preferred_element_type=jnp.float32,
    )
    local_keys = rotate_pairs(projected[:, None, :head_dim], positions)[:, 0]
    key_value = jnp.concatenate([local_keys, projected[:, head_dim:]], axis=1).astype(jnp.bfloat16)
    group_kv = lax.all_gather(key_value, "seq", axis=0, tiled=True)
    span = group_kv.shape[0]
    reach = span // 4
    earlier = shifted(group_kv[span - reach :], "dp", 1)
    window = jnp.concatenate([earlier, group_kv], axis=0)
    group_index = lax.axis_index("dp")
    my_index = lax.axis_index("seq")
    window_start = group_index * span - reach
    rotated = rotate_pairs(
        queries.astype(jnp.float32).reshape(local_count, GROUP, head_dim), positions
    ).astype(jnp.bfloat16)
    offset = my_index * local_count
    near = lax.dynamic_slice_in_dim(window, offset, reach + local_count, 0)
    key_global = window_start + offset + jnp.arange(reach + local_count, dtype=jnp.int32)
    query_global = jnp.repeat(
        group_index * span + offset + jnp.arange(local_count, dtype=jnp.int32), GROUP
    )
    query_places = jnp.repeat(positions, GROUP)
    results = attend_rows(
        rotated.reshape(local_count * GROUP, head_dim),
        query_global,
        query_places,
        near[:, :head_dim],
        near[:, head_dim:],
        key_global,
    )
    attention = results.reshape(local_count, GROUP * head_dim)
    return (attention, new_master, new_first, new_second)


def solution(mesh):
    return jax.shard_map(
        local,
        mesh=mesh,
        in_specs=(
            P(("dp", "seq"), None),
            P(("dp", "seq"), None),
            P(("dp", "seq")),
            P(("dp", "seq"), None),
            P(("dp", "seq"), None),
            P(("dp", "seq"), None),
            P(("dp", "seq"), None),
            P(),
        ),
        out_specs=(
            P(("dp", "seq"), None),
            P(("dp", "seq"), None),
            P(("dp", "seq"), None),
            P(("dp", "seq"), None),
        ),
        check_vma=False,
    )
```

profile of v0, /device:TPU:9, one launch (start us, length us, event | category | flops | bytes accessed | tf_op | source)
XLA Modules:
  0.0 108.6 jit_solution(13167087772122464027)
XLA Ops:
  8.1 2.2 %fusion.19 = (bf16[256,256]{1,0:T(8,128)(2,1)}, f32[256,256]{1,0:T(8,128)}, f32[256,256]{1,0:T(8,128)}, f32[256,256]{1,0:T(8,128)}) fusion(f32[256,256]{1,0:T(8,128)} %param.14, f32[]{:T(128)} %bitcast.3, f32[]{:T(128)} %bitcast.2, f32[256,256]{1,0:T(8,128)} %param.13, f32[256,256]{1,0:T(8,128)} %param.15, f32[256,256]{1,0:T(8,128)} %param.16), kind=kLoop, calls=%fused_computation.45 | loop fusion | flops 917504 | bytes 1966088 | tf_op jit(solution)/shard_map/convert_element_type | solution.py:83
  10.3 0.7 convert_element_type.21
  11.0 1.0 convert_bitcast_fusion
  12.1 0.3 multiply_cosine_fusion
  12.4 0.3 subtract_convert_fusion
  12.7 62.3 %all-gather.2.cloned.1.call-done = bf16[8192,256]{1,0:T(8,128)(2,1)} async-done(((bf16[256,256]{1,0:T(8,128)(2,1)}), bf16[8192,256]{1,0:T(8,128)(2,1)}) %all-gather.2.cloned.1.call-update) | async-done | bytes 4194320 | tf_op jit(solution)/shard_map/all_gather | solution.py:88
  75.1 3.5 %convolution_bitcast_fusion = f32[128,256]{0,1:T(8,128)S(1)} fusion(bf16[8192,256]{1,0:T(8,128)(2,1)} %all-gather.2.cloned.1.call-done, bf16[128,8192]{1,0:T(8,128)(2,1)S(1)} %copy-done), kind=kOutput, calls=%fused_computation.15 | convolution fusion | flops 536870912 | bytes 6422528 | tf_op jit(solution)/shard_map/dot_general | solution.py:86
  78.5 0.2 fusion.16
  78.8 10.0 %all_gather.7 = bf16[1024,256]{0,1:T(8,128)(2,1)S(1)} all-gather(bf16[128,256]{0,1:T(8,128)(2,1)S(1)} %pad_maximum_fusion.1), channel_id=1, replica_groups=mesh['dp'=4,'seq'=8] {'seq'}, dimensions={0}, use_global_device_ids=true | all-gather | bytes 589824 | tf_op jit(solution)/shard_map/all_gather | solution.py:93
  88.9 2.4 %collective-permute-start = (bf16[256,256]{0,1:T(8,128)(2,1)S(1)}, bf16[256,256]{0,1:T(8,128)(2,1)}, u32[]{:S(2)}, u32[]{:S(2)}) collective-permute-start(bf16[256,256]{0,1:T(8,128)(2,1)S(1)} %slice.43), channel_id=1, source_target_pairs={{0,8},{8,16},{16,24},{1,9},{9,17},{17,25},{2,10},{10,18},{18,26},{... | collective-permute-start | bytes 393224 | tf_op jit(solution)/shard_map/ppermute | solution.py:22
  91.4 0.1 broadcast_in_dim.38
  91.7 0.1 pad_maximum_fusion
  91.9 3.9 %collective-permute-done = bf16[256,256]{0,1:T(8,128)(2,1)} collective-permute-done((bf16[256,256]{0,1:T(8,128)(2,1)S(1)}, bf16[256,256]{0,1:T(8,128)(2,1)}, u32[]{:S(2)}, u32[]{:S(2)}) %collective-permute-start) | collective-permute-done | bytes 131104 | tf_op jit(solution)/shard_map/ppermute | solution.py:22
  95.8 0.9 fusion.10
  96.8 0.1 copy.14
  96.9 0.1 copy.15
  97.0 3.0 %while.11 = (s32[]{:T(128)}, bf16[2,512,128]{2,1,0:T(8,128)(2,1)}, s32[2,512]{1,0:T(2,128)S(1)}, s32[2,512]{1,0:T(2,128)S(1)}, bf16[2,512,128]{2,1,0:T(8,128)(2,...) while((s32[]{:T(128)}, bf16[2,512,128]{2,1,0:T(8,128)(2,1)}, ...), condition=%wide.region_3.4_spmd.clone, body=%wide.region_0.3_spmd.clone.sunk | while | flops 102891392 | bytes 2850921 | solution.py:70
  97.1 0.3 fusion.34
  97.4 0.2 fusion.35
  97.5 1.0 fusion.36
  98.6 0.3 fusion.34
  98.9 0.2 fusion.35
  99.0 1.0 fusion.36
  100.0 1.8 %reshape_reshape.2 = bf16[128,1024]{1,0:T(8,128)(2,1)} reshape(bf16[2,512,128]{2,1,0:T(8,128)(2,1)} %get-tuple-element.46) | data formatting | bytes 524288 | tf_op jit(solution)/shard_map/reshape;reshape | solution.py:119
  (26 shorter events, 0.6 us)
Async XLA Ops:
  7.2 67.9 %copy-start = (bf16[128,8192]{1,0:T(8,128)(2,1)S(1)}, bf16[128,8192]{1,0:T(8,128)(2,1)}, u32[]{:S(2)}) copy-start(bf16[128,8192]{1,0:T(8,128)(2,1)} %param.10) | copy-start | bytes 6291460
  7.2 67.9 %all-gather.2.cloned.1.call-start = ((), (), s32[]{:S(2)}) async-start(), calls=%async_computation | async-start | bytes 4325376 | tf_op jit(solution)/shard_map/all_gather | solution.py:88
  12.7 78.6 %copy-start.1 = (s32[128]{0:T(128)S(1)}, s32[128]{0:T(128)}, u32[]{:S(2)}) copy-start(s32[128]{0:T(128)} %param.12) | copy-start | bytes 1540
  88.9 7.0 %collective-permute-start = (bf16[256,256]{0,1:T(8,128)(2,1)S(1)}, bf16[256,256]{0,1:T(8,128)(2,1)}, u32[]{:S(2)}, u32[]{:S(2)}) collective-permute-start(bf16[256,256]{0,1:T(8,128)(2,1)S(1)} %slice.43), channel_id=1, source_target_pairs={{0,8},{8,16},{16,24},{1,9},{9,17},{17,25},{2,10},{10,18},{18,26},{... | collective-permute-start | bytes 393224 | tf_op jit(solution)/shard_map/ppermute | solution.py:22
Sparse Core Ops, SparseCore 0:
  11.4 63.5 all-gather.1
where the time goes:
time: 110 us; the launch traced here: 109 us
  waiting for transfers between devices  66.3 us (60%)
  between operations  15.1 us (14%)
  blocking collectives  10 us (9%)
  matrix products  6.08 us (6%)
  other arithmetic  6.03 us (5%)
  local copies, waits for them, and re-layouts  2.63 us (2%)
  starting transfers between devices  2.42 us (2%)
    all_gather x1, waiting for transfers between devices, local(): lax.all_gather(weight, ('dp', 'seq'), axis=0, tiled=True)  62.3 us
    all_gather x1, blocking collectives, local(): group_kv = lax.all_gather(key_value, 'seq', axis=0, tiled=True)  10 us
    ppermute x1, waiting for transfers between devices, shifted(): lax.ppermute(value, axis, [(source, source + steps) for source in range(f...  3.92 us
    dot_general x1, matrix products, local(): jnp.dot(tokens, lax.all_gather(weight, ('dp', 'seq'), axis=0, tiled=True)...  3.46 us
    ppermute x1, starting transfers between devices, shifted(): lax.ppermute(value, axis, [(source, source + steps) for source in range(f...  2.38 us
  transfers between devices with their start and end apart: 2, of which 2 were waited for; matrix products, arithmetic and copies ran while one was open for 3% of the time, Pallas kernels for 0%

commit v1 on v0

--- a/solution.py
+++ b/solution.py
@@ -3,9 +3,12 @@
 import jax
 import jax.numpy as jnp
 from jax import lax
+from jax.experimental import pallas as pl
+from jax.experimental.pallas import tpu as pltpu
 from jax.sharding import PartitionSpec as P
 
 GROUP = 8
+MESH = pl.DeviceIdType.MESH
 
 
 beta_one = 0.9
@@ -120,9 +123,313 @@
     return (attention, new_master, new_first, new_second)
 
 
+def rope_tables(places, width):
+    lane = lax.broadcasted_iota(jnp.int32, (1, width), 1)
+    half_width = width // 2
+    slot = jnp.where(lane < half_width, lane, lane - half_width).astype(jnp.float32)
+    freqs = jnp.exp(slot * (-2.0 * math.log(rope_base) / width))
+    angles = places.astype(jnp.float32) * freqs
+    sine = jnp.sin(angles)
+    return jnp.cos(angles), jnp.where(lane < half_width, -sine, sine)
+
+
+def fused_kernel(
+    tok_hbm, query_hbm, weight_ref, places_ref, out_ref,
+    tok, blocks, query, rotated, part, back, kv, cosine, sine,
+    tok_sem, tok_send, tok_recv, query_sem, block_recv, half_recv,
+    x_send, y_send, z_send, cross_send, half_x_send, half_y_send,
+    back_sems, kv_send, kv_recv,
+):
+    z = lax.axis_index("dp")
+    seq = lax.axis_index("seq")
+    planes = lax.axis_size("dp")
+    wide = lax.axis_size("seq")
+    core = lax.rem(seq, 2)
+    x = lax.rem(seq // 2, 2)
+    y = seq // 4
+    count = tok_hbm.shape[0]
+    depth = weight_ref.shape[0]
+    half = depth // 2
+    head_dim = weight_ref.shape[1] // 2
+    me = z * wide + seq
+    total = planes * wide
+    chips = blocks.shape[0]
+
+    def ordinal(index):
+        return (index // wide, lax.rem(index, wide))
+
+    peer = (z, seq + 1 - 2 * core)
+    x_side = (z, seq + 2 - 4 * x)
+    y_side = (z, seq + 4 - 8 * y)
+    z_pair = z + 1 - 2 * lax.rem(z, 2)
+    pair_side = (z_pair, seq)
+    cross_side = (3 - z, seq)
+    inner = (z == 1) | (z == 2)
+    next_one, next_two = lax.rem(me + 1, total), lax.rem(me + 2, total)
+    last_one, last_two = lax.rem(me + total - 1, total), lax.rem(me + total - 2, total)
+
+    barrier = pltpu.get_barrier_semaphore()
+    greeted = [peer, x_side, y_side, pair_side, cross_side]
+    greeted += [ordinal(index) for index in (next_one, next_two, last_one, last_two)]
+    for device in greeted:
+        pl.semaphore_signal(barrier, inc=1, device_id=device, device_id_type=MESH)
+
+    def columns(chip, which):
+        return pl.ds(pl.multiple_of((chip * 2 + which) * depth, depth), depth)
+
+    def rows_of(which):
+        return pl.ds(pl.multiple_of(which * count, count), count)
+
+    def local_tokens(chip):
+        return pltpu.make_async_copy(
+            tok_hbm.at[:, columns(chip, core)], tok.at[chip, rows_of(core)], tok_sem.at[chip]
+        )
+
+    def sent_tokens(chip):
+        return pltpu.make_async_remote_copy(
+            src_ref=tok_hbm.at[:, columns(chip, 1 - core)],
+            dst_ref=tok.at[chip, rows_of(core)],
+            send_sem=tok_send.at[chip],
+            recv_sem=tok_recv.at[chip],
+            device_id=peer,
+            device_id_type=MESH,
+        )
+
+    query_copy = pltpu.make_async_copy(query_hbm, query, query_sem)
+    pl.semaphore_wait(barrier, len(greeted))
+
+    order = [z, z_pair, 2 - z // 2, 3 - 3 * (z // 2)]
+
+    def chip_at(plane, y_at, x_at):
+        return plane * 4 + y_at * 2 + x_at
+
+    def send_block(step, device, sem):
+        chip = chip_at(order[step], y, x)
+        return pltpu.make_async_remote_copy(
+            src_ref=weight_ref if step == 0 else blocks.at[chip],
+            dst_ref=blocks.at[chip],
+            send_sem=sem.at[step],
+            recv_sem=block_recv.at[chip],
+            device_id=device,
+            device_id_type=MESH,
+        )
+
+    def send_half(step, which):
+        chip = chip_at(order[step], y, 1 - x) if which == 0 else chip_at(order[step], 1 - y, x)
+        return pltpu.make_async_remote_copy(
+            src_ref=blocks.at[chip, pl.ds(which * half, half)],
+            dst_ref=blocks.at[chip, pl.ds(which * half, half)],
+            send_sem=(half_y_send if which == 0 else half_x_send).at[step],
+            recv_sem=half_recv.at[which, chip],
+            device_id=y_side if which == 0 else x_side,
+            device_id_type=MESH,
+        )
+
+    def block_arrival(chip):
+        pltpu.make_async_copy(blocks.at[chip], blocks.at[chip], block_recv.at[chip]).wait()
+
+    def half_arrival(which, chip):
+        place = blocks.at[chip, pl.ds(which * half, half)]
+        pltpu.make_async_copy(place, place, half_recv.at[which, chip]).wait()
+
+    def add_block(chip, source):
+        local_tokens(chip).wait()
+        sent_tokens(chip).wait_recv()
+        part[...] += jnp.dot(tok[chip], source[...], preferred_element_type=jnp.float32)
+
+    steps = len(order)
+    for device, sem in ((x_side, x_send), (y_side, y_send), (pair_side, z_send)):
+        send_block(0, device, sem).start()
+
+    @pl.when(inner)
+    def _():
+        send_block(0, cross_side, cross_send).start()
+
+    query_copy.start()
+
+    @pl.loop(0, chips)
+    def _(chip):
+        sent_tokens(chip).start()
+        local_tokens(chip).start()
+
+    part[...] = jnp.zeros_like(part)
+
+    row = lax.broadcasted_iota(jnp.int32, (count, count), 0)
+    lane = lax.broadcasted_iota(jnp.int32, (count, count), 1)
+    places = jnp.sum(
+        jnp.where(row == lane, places_ref[...].astype(jnp.float32), 0.0), axis=1, keepdims=True
+    )
+    cosine[...], sine[...] = rope_tables(places, head_dim)
+
+    def rotate(values_in):
+        return values_in * cosine[...] + pltpu.roll(values_in, head_dim // 2, 1) * sine[...]
+
+    query_copy.wait()
+    heads = query.shape[1] // head_dim
+    for head in range(heads):
+        at = slice(head * head_dim, (head + 1) * head_dim)
+        rotated[:, at] = rotate(query[:, at].astype(jnp.float32)).astype(jnp.bfloat16)
+    add_block(chip_at(z, y, x), weight_ref)
+
+    for step in range(1, steps + 1):
+        if step < steps:
+            chip = chip_at(order[step], y, x)
+            block_arrival(chip)
+
+            @pl.when(inner)
+            def _():
+                if step == 1:
+                    send_block(step, cross_side, cross_send).start()
+                else:
+                    send_block(step, pair_side, z_send).start()
+
+            send_block(step, x_side, x_send).start()
+            send_block(step, y_side, y_send).start()
+            add_block(chip, blocks.at[chip])
+        across = [chip_at(order[step - 1], y, 1 - x), chip_at(order[step - 1], 1 - y, x)]
+        for which in range(2):
+            block_arrival(across[which])
+            send_half(step - 1, which).start()
+        for chip in across:
+            add_block(chip, blocks.at[chip])
+        if step > 1:
+            chip = chip_at(order[step - 2], 1 - y, 1 - x)
+            half_arrival(0, chip)
+            half_arrival(1, chip)
+            add_block(chip, blocks.at[chip])
+    chip = chip_at(order[steps - 1], 1 - y, 1 - x)
+    half_arrival(0, chip)
+    half_arrival(1, chip)
+    add_block(chip, blocks.at[chip])
+
+    back_copy = pltpu.make_async_remote_copy(
+        src_ref=part.at[rows_of(1 - core)],
+        dst_ref=back,
+        send_sem=back_sems.at[0],
+        recv_sem=back_sems.at[1],
+        device_id=peer,
+        device_id_type=MESH,
+    )
+    back_copy.start()
+    back_copy.wait_recv()
+    projected = part[rows_of(core)] + back[...]
+    own = pl.ds(2 * count, count)
+    kv[own, :head_dim] = rotate(projected[:, :head_dim]).astype(jnp.bfloat16)
+    kv[own, head_dim:] = projected[:, head_dim:].astype(jnp.bfloat16)
+
+    def send_kv(distance):
+        return pltpu.make_async_remote_copy(
+            src_ref=kv.at[own],
+            dst_ref=kv.at[pl.ds((2 - distance) * count, count)],
+            send_sem=kv_send.at[distance - 1],
+            recv_sem=kv_recv.at[distance - 1],
+            device_id=ordinal(next_one if distance == 1 else next_two),
+            device_id_type=MESH,
+        )
+
+    for distance in (1, 2):
+
+        @pl.when(me < total - distance)
+        def _():
+            send_kv(distance).start()
+
+        @pl.when(me < distance)
+        def _():
+            kv[pl.ds((2 - distance) * count, count), :] = jnp.zeros(
+                (count, 2 * head_dim), jnp.bfloat16
+            )
+
+    key_row = lax.broadcasted_iota(jnp.int32, (count, 3 * count), 1) - 2 * count
+    query_row = lax.broadcasted_iota(jnp.int32, (count, 3 * count), 0)
+    allowed = (key_row <= query_row) & (key_row >= query_row - places.astype(jnp.int32))
+
+    for distance in (1, 2):
+
+        @pl.when(me >= distance)
+        def _():
+            send_kv(distance).wait_recv()
+
+    keys = kv[:, :head_dim]
+    values_v = kv[:, head_dim:]
+    for head in range(heads):
+        at = slice(head * head_dim, (head + 1) * head_dim)
+        scores = lax.dot_general(
+            rotated[:, at], keys, (((1,), (1,)), ((), ())), preferred_element_type=jnp.float32
+        ) * head_dim ** (-0.5)
+        scores = jnp.where(allowed, scores, masked_score)
+        weights = jnp.exp(scores - jnp.max(scores, axis=1, keepdims=True))
+        probs = (weights * (1.0 / jnp.sum(weights, axis=1, keepdims=True))).astype(jnp.bfloat16)
+        out_ref[:, at] = jnp.dot(probs, values_v, preferred_element_type=jnp.float32).astype(
+            jnp.bfloat16
+        )
+
+    for step in range(steps):
+        send_block(step, x_side, x_send).wait_send()
+        send_block(step, y_side, y_send).wait_send()
+        send_half(step, 0).wait_send()
+        send_half(step, 1).wait_send()
+    send_block(0, pair_side, z_send).wait_send()
+
+    @pl.when(inner)
+    def _():
+        send_block(2, pair_side, z_send).wait_send()
+        send_block(3, pair_side, z_send).wait_send()
+        send_block(0, cross_side, cross_send).wait_send()
+        send_block(1, cross_side, cross_send).wait_send()
+
+    @pl.loop(0, chips)
+    def _(chip):
+        sent_tokens(chip).wait_send()
+
+    back_copy.wait_send()
+    for distance in (1, 2):
+
+        @pl.when(me < total - distance)
+        def _():
+            send_kv(distance).wait_send()
+
+
+def fused_local(tokens, queries, positions, grad, master, moment1, moment2, step):
+    new_master, new_first, new_second = adam_update(grad, master, moment1, moment2, step)
+    weight = new_master.astype(jnp.bfloat16)
+    count = tokens.shape[0]
+    depth, width = weight.shape
+    head_dim = width // 2
+    chips = tokens.shape[1] // depth // 2
+    dma = pltpu.SemaphoreType.DMA
+    anywhere = pl.BlockSpec(memory_space=pl.ANY)
+    inside = pl.BlockSpec(memory_space=pltpu.VMEM)
+    attention = pl.pallas_call(
+        fused_kernel,
+        out_shape=jax.ShapeDtypeStruct(queries.shape, jnp.bfloat16),
+        in_specs=[anywhere, anywhere, inside, inside],
+        out_specs=inside,
+        scratch_shapes=[
+            pltpu.VMEM((chips, 2 * count, depth), jnp.bfloat16),
+            pltpu.VMEM((chips, depth, width), jnp.bfloat16),
+            pltpu.VMEM(queries.shape, jnp.bfloat16),
+            pltpu.VMEM(queries.shape, jnp.bfloat16),
+            pltpu.VMEM((2 * count, width), jnp.float32),
+            pltpu.VMEM((count, width), jnp.float32),
+            pltpu.VMEM((3 * count, width), jnp.bfloat16),
+            pltpu.VMEM((count, head_dim), jnp.float32),
+            pltpu.VMEM((count, head_dim), jnp.float32),
+            dma((chips,)), dma((chips,)), dma((chips,)), dma,
+            dma((chips,)), dma((2, chips)),
+            dma((4,)), dma((4,)), dma((4,)), dma((4,)), dma((4,)), dma((4,)),
+            dma((2,)), dma((2,)), dma((2,)),
+        ],
+        compiler_params=pltpu.CompilerParams(
+            collective_id=0, has_side_effects=True, vmem_limit_bytes=40 * 1024 * 1024
+        ),
+    )(tokens, queries, weight, positions.reshape(1, -1))
+    return (attention, new_master, new_first, new_second)
+
+
 def solution(mesh):
+    small = (mesh.shape["dp"], mesh.shape["seq"]) == (4, 8)
     return jax.shard_map(
-        local,
+        fused_local if small else local,
         mesh=mesh,
         in_specs=(
             P(("dp", "seq"), None),

time: 110 us -> 44 us (0.40)
  waiting for transfers between devices: 66.3 us -> 0 us
  Pallas kernels: 0 us -> 36.8 us
  between operations: 15.1 us -> 1.42 us
  blocking collectives: 10 us -> 0 us
  matrix products: 6.08 us -> 0 us
  other arithmetic: 6.03 us -> 2.15 us
  starting transfers between devices: 2.42 us -> 0 us
    all_gather x1 -> x0, waiting for transfers between devices: 62.3 us -> none  [local(): lax.all_gather(weight, ('dp', 'seq'), axis=0, tiled=True)]
    pallas_call x0 -> x1, Pallas kernels: none -> 36.8 us  [fused_local(): pl.pallas_call(fused_kernel, out_shape=jax.ShapeDtypeStruct(queries.shape...]
    all_gather x1 -> x0, blocking collectives: 10 us -> none  [local(): group_kv = lax.all_gather(key_value, 'seq', axis=0, tiled=True)]
    dot_general x5 -> x0, matrix products: 6.08 us -> none  [the longest x1 3.46 us: local(): jnp.dot(tokens, lax.all_gather(weight, ('dp', 'seq'), axis=0, tiled=True)...]
    ppermute x1 -> x0, waiting for transfers between devices: 3.92 us -> none  [shifted(): lax.ppermute(value, axis, [(source, source + steps) for source in range(f...]
    unnamed x7, local copies, waits for them, and re-layouts: 0.36 us -> 2.96 us
    ppermute x1 -> x0, starting transfers between devices: 2.38 us -> none  [shifted(): lax.ppermute(value, axis, [(source, source + steps) for source in range(f...]
    another operation x1 -> x0, local copies, waits for them, and re-layouts: 1.77 us -> none  [local(): attention = results.reshape(local_count, GROUP * head_dim)]
  transfers between devices with their start and end apart: 2 -> 0, of which waited for: 2 -> 0; matrix products, arithmetic and copies ran while one was open for 3% -> 0% of each run, Pallas kernels for 0% -> 0%
where the time goes in v1:
time: 44 us; the launch traced here: 43.4 us
  Pallas kernels  36.8 us (84%)
  local copies, waits for them, and re-layouts  2.96 us (7%)
  other arithmetic  2.15 us (5%)
  between operations  1.42 us (3%)
    pallas_call x1, Pallas kernels, fused_local(): pl.pallas_call(fused_kernel, out_shape=jax.ShapeDtypeStruct(queries.shape...  36.8 us
    unnamed x7, local copies, waits for them, and re-layouts  2.96 us
    convert_element_type x1, other arithmetic, fused_local(): weight = new_master.astype(jnp.bfloat16)  2.15 us

profile of v1, /device:TPU:9, one launch (start us, length us, event | category | flops | bytes accessed | tf_op | source)
XLA Modules:
  0.0 43.4 jit_solution(8799933011524796093)
XLA Ops:
  0.6 0.0 copy-start.1
  1.4 2.2 %fusion.1 = (bf16[256,256]{1,0:T(8,128)(2,1)S(1)}, f32[256,256]{1,0:T(8,128)}, f32[256,256]{1,0:T(8,128)}, f32[256,256]{1,0:T(8,128)}) fusion(f32[256,256]{1,0:T(8,128)} %param.12, f32[]{:T(128)} %bitcast.1, f32[]{:T(128)} %bitcast, f32[256,256]{1,0:T(8,128)} %param.11, f32[256,256]{1,0:T(8,128)} %param.13, f32[256,256]{1,0:T(8,128)} %param.14), kind=kLoop, calls=%fused_computation.4 | loop fusion | flops 917504 | bytes 1966088 | tf_op jit(solution)/shard_map/convert_element_type | solution.py:394
  3.6 0.0 copy-done.1
  3.6 0.0 copy-start
  3.6 1.6 %copy-done = bf16[128,8192]{1,0:T(8,128)(2,1)S(1)} copy-done((bf16[128,8192]{1,0:T(8,128)(2,1)S(1)}, bf16[128,8192]{1,0:T(8,128)(2,1)}, u32[]{:S(2)}) %copy-start) | copy-done | bytes 2097176
  5.2 0.0 copy-start.2
  5.2 0.7 %copy-done.2 = s32[128]{0:T(128)S(1)} copy-done((s32[128]{0:T(128)S(1)}, s32[128]{0:T(128)}, u32[]{:S(2)}) %copy-start.2) | copy-done | bytes 536
  5.8 36.8 %shard_map.111 = bf16[128,1024]{1,0:T(8,128)(2,1)S(1)} custom-call(bf16[128,8192]{1,0:T(8,128)(2,1)S(1)} %copy-done, bf16[128,1024]{1,0:T(8,128)(2,1)S(1)} %copy-done.1, bf16[256,256]{1,0:T(8,128)(2,1)S(1)} %get-tuple-element.4.weight_ref, s32[1,128]{1,0:T(1,128)S(1)} %bitcast.3), custom_call_target="tpu_custom_call" | custom-call | tf_op jit(solution)/shard_map/pallas_call | solution.py:402
  42.6 0.7 %copy.14 = bf16[128,1024]{1,0:T(8,128)(2,1)} copy(bf16[128,1024]{1,0:T(8,128)(2,1)S(1)} %shard_map.111) | data formatting | bytes 524288
Async XLA Ops:
  0.6 2.9 %copy-start.1 = (bf16[128,1024]{1,0:T(8,128)(2,1)S(1)}, bf16[128,1024]{1,0:T(8,128)(2,1)}, u32[]{:S(2)}) copy-start(bf16[128,1024]{1,0:T(8,128)(2,1)} %query_hbm.1) | copy-start | bytes 786436
  3.6 1.6 %copy-start = (bf16[128,8192]{1,0:T(8,128)(2,1)S(1)}, bf16[128,8192]{1,0:T(8,128)(2,1)}, u32[]{:S(2)}) copy-start(bf16[128,8192]{1,0:T(8,128)(2,1)} %tok_hbm.1) | copy-start | bytes 6291460
  5.2 0.7 %copy-start.2 = (s32[128]{0:T(128)S(1)}, s32[128]{0:T(128)}, u32[]{:S(2)}) copy-start(s32[128]{0:T(128)} %param.10) | copy-start | bytes 1540

commit v2 on v1

--- a/solution.py
+++ b/solution.py
@@ -134,10 +134,10 @@
 
 
 def fused_kernel(
-    tok_hbm, query_hbm, weight_ref, places_ref, out_ref,
-    tok, blocks, query, rotated, part, back, kv, cosine, sine,
-    tok_sem, tok_send, tok_recv, query_sem, block_recv, half_recv,
-    x_send, y_send, z_send, cross_send, half_x_send, half_y_send,
+    tok_hbm, query_hbm, weight_ref, places_hbm, out_ref,
+    places_ref, own_scores, tok, blocks, query, rotated, part, back, kv, cosine, sine,
+    tok_sem, tok_send, tok_recv, query_sem, places_sem, block_recv, half_recv,
+    x_send, y_send, z_send, cross_send, half_x_send, half_y_send, across_send,
     back_sems, kv_send, kv_recv,
 ):
     z = lax.axis_index("dp")
@@ -196,6 +196,9 @@
         )
 
     query_copy = pltpu.make_async_copy(query_hbm, query, query_sem)
+    places_copy = pltpu.make_async_copy(places_hbm, places_ref, places_sem)
+    query_copy.start()
+    places_copy.start()
     pl.semaphore_wait(barrier, len(greeted))
 
     order = [z, z_pair, 2 - z // 2, 3 - 3 * (z // 2)]
@@ -225,6 +228,17 @@
             device_id_type=MESH,
         )
 
+    def send_across(step, device, sem):
+        chip = chip_at(order[step], 1 - y, 1 - x)
+        return pltpu.make_async_remote_copy(
+            src_ref=blocks.at[chip],
+            dst_ref=blocks.at[chip],
+            send_sem=sem,
+            recv_sem=block_recv.at[chip],
+            device_id=device,
+            device_id_type=MESH,
+        )
+
     def block_arrival(chip):
         pltpu.make_async_copy(blocks.at[chip], blocks.at[chip], block_recv.at[chip]).wait()
 
@@ -245,8 +259,6 @@
     def _():
         send_block(0, cross_side, cross_send).start()
 
-    query_copy.start()
-
     @pl.loop(0, chips)
     def _(chip):
         sent_tokens(chip).start()
@@ -254,6 +266,7 @@
 
     part[...] = jnp.zeros_like(part)
 
+    places_copy.wait()
     row = lax.broadcasted_iota(jnp.int32, (count, count), 0)
     lane = lax.broadcasted_iota(jnp.int32, (count, count), 1)
     places = jnp.sum(
@@ -264,43 +277,78 @@
     def rotate(values_in):
         return values_in * cosine[...] + pltpu.roll(values_in, head_dim // 2, 1) * sine[...]
 
+    own_chip = chip_at(z, y, x)
+    line = [chip_at(plane, y, x) for plane in order]
+    along_x = [chip_at(plane, y, 1 - x) for plane in order]
+    along_y = [chip_at(plane, 1 - y, x) for plane in order]
+    corner = [chip_at(plane, 1 - y, 1 - x) for plane in order]
+
+    def add_blocks(*chips_in):
+        for chip in chips_in:
+            add_block(chip, blocks.at[chip])
+
+    def forward_halves(step):
+        for which, chip in enumerate((along_x[step], along_y[step])):
+            block_arrival(chip)
+            send_half(step, which).start()
+
+    def forward_line(step):
+        block_arrival(line[step])
+
+        @pl.when(inner)
+        def _():
+            if step == 1:
+                send_block(step, cross_side, cross_send).start()
+            else:
+                send_block(step, pair_side, z_send).start()
+
+        send_block(step, x_side, x_send).start()
+        send_block(step, y_side, y_send).start()
+
     query_copy.wait()
     heads = query.shape[1] // head_dim
+    add_block(own_chip, weight_ref)
+    forward_halves(0)
+    forward_line(1)
+    forward_line(2)
+    half_arrival(0, corner[0])
+    half_arrival(1, corner[0])
+    send_across(0, pair_side, across_send.at[0]).start()
+
+    @pl.when(inner)
+    def _():
+        send_across(0, cross_side, across_send.at[1]).start()
+
     for head in range(heads):
         at = slice(head * head_dim, (head + 1) * head_dim)
         rotated[:, at] = rotate(query[:, at].astype(jnp.float32)).astype(jnp.bfloat16)
-    add_block(chip_at(z, y, x), weight_ref)
-
-    for step in range(1, steps + 1):
-        if step < steps:
-            chip = chip_at(order[step], y, x)
-            block_arrival(chip)
-
-            @pl.when(inner)
-            def _():
-                if step == 1:
-                    send_block(step, cross_side, cross_send).start()
-                else:
-                    send_block(step, pair_side, z_send).start()
-
-            send_block(step, x_side, x_send).start()
-            send_block(step, y_side, y_send).start()
-            add_block(chip, blocks.at[chip])
-        across = [chip_at(order[step - 1], y, 1 - x), chip_at(order[step - 1], 1 - y, x)]
-        for which in range(2):
-            block_arrival(across[which])
-            send_half(step - 1, which).start()
-        for chip in across:
-            add_block(chip, blocks.at[chip])
-        if step > 1:
-            chip = chip_at(order[step - 2], 1 - y, 1 - x)
-            half_arrival(0, chip)
-            half_arrival(1, chip)
-            add_block(chip, blocks.at[chip])
-    chip = chip_at(order[steps - 1], 1 - y, 1 - x)
-    half_arrival(0, chip)
-    half_arrival(1, chip)
-    add_block(chip, blocks.at[chip])
+    forward_line(3)
+    add_blocks(along_x[0], along_y[0], line[1])
+
+    @pl.when(inner)
+    def _():
+        block_arrival(corner[2])
+        send_across(2, pair_side, across_send.at[2]).start()
+
+    add_blocks(line[2], corner[0])
+    block_arrival(along_x[1])
+    block_arrival(along_y[1])
+    add_blocks(along_x[1], along_y[1])
+    block_arrival(along_x[2])
+    block_arrival(along_y[2])
+    forward_halves(3)
+    add_blocks(along_x[2], along_y[2], line[3], along_x[3], along_y[3])
+    block_arrival(corner[1])
+    add_blocks(corner[1])
+
+    @pl.when((z == 0) | (z == 3))
+    def _():
+        block_arrival(corner[2])
+
+    add_blocks(corner[2])
+    half_arrival(0, corner[3])
+    half_arrival(1, corner[3])
+    add_blocks(corner[3])
 
     back_copy = pltpu.make_async_remote_copy(
         src_ref=part.at[rows_of(1 - core)],
@@ -339,9 +387,23 @@
                 (count, 2 * head_dim), jnp.bfloat16
             )
 
-    key_row = lax.broadcasted_iota(jnp.int32, (count, 3 * count), 1) - 2 * count
-    query_row = lax.broadcasted_iota(jnp.int32, (count, 3 * count), 0)
-    allowed = (key_row <= query_row) & (key_row >= query_row - places.astype(jnp.int32))
+    near_limit = row - places.astype(jnp.int32)
+    early = lax.broadcasted_iota(jnp.int32, (count, 2 * count), 1) - 2 * count
+    allowed_own = (lane <= row) & (lane >= near_limit)
+    allowed_early = early >= near_limit[:, :1]
+
+    def score(head, keys, allowed):
+        scores = lax.dot_general(
+            rotated[:, head * head_dim : (head + 1) * head_dim],
+            keys,
+            (((1,), (1,)), ((), ())),
+            preferred_element_type=jnp.float32,
+        ) * head_dim ** (-0.5)
+        return jnp.where(allowed, scores, masked_score)
+
+    own_keys = kv[own, :head_dim]
+    for head in range(heads):
+        own_scores[head] = score(head, own_keys, allowed_own)
 
     for distance in (1, 2):
 
@@ -349,26 +411,37 @@
         def _():
             send_kv(distance).wait_recv()
 
-    keys = kv[:, :head_dim]
-    values_v = kv[:, head_dim:]
+    past = pl.ds(0, 2 * count)
+    early_keys = kv[past, :head_dim]
+    early_values = kv[past, head_dim:]
+    own_values = kv[own, head_dim:]
     for head in range(heads):
         at = slice(head * head_dim, (head + 1) * head_dim)
-        scores = lax.dot_general(
-            rotated[:, at], keys, (((1,), (1,)), ((), ())), preferred_element_type=jnp.float32
-        ) * head_dim ** (-0.5)
-        scores = jnp.where(allowed, scores, masked_score)
-        weights = jnp.exp(scores - jnp.max(scores, axis=1, keepdims=True))
-        probs = (weights * (1.0 / jnp.sum(weights, axis=1, keepdims=True))).astype(jnp.bfloat16)
-        out_ref[:, at] = jnp.dot(probs, values_v, preferred_element_type=jnp.float32).astype(
-            jnp.bfloat16
-        )
+        near = own_scores[head]
+        far = score(head, early_keys, allowed_early)
+        top = jnp.maximum(
+            jnp.max(near, axis=1, keepdims=True), jnp.max(far, axis=1, keepdims=True)
+        )
+        near = jnp.exp(near - top)
+        far = jnp.exp(far - top)
+        share = 1.0 / (
+            jnp.sum(near, axis=1, keepdims=True) + jnp.sum(far, axis=1, keepdims=True)
+        )
+        result = jnp.dot(
+            (near * share).astype(jnp.bfloat16), own_values, preferred_element_type=jnp.float32
+        ) + jnp.dot(
+            (far * share).astype(jnp.bfloat16), early_values, preferred_element_type=jnp.float32
+        )
+        out_ref[:, at] = result.astype(jnp.bfloat16)
 
     for step in range(steps):
         send_block(step, x_side, x_send).wait_send()
         send_block(step, y_side, y_send).wait_send()
+    for step in (0, 3):
         send_half(step, 0).wait_send()
         send_half(step, 1).wait_send()
     send_block(0, pair_side, z_send).wait_send()
+    send_across(0, pair_side, across_send.at[0]).wait_send()
 
     @pl.when(inner)
     def _():
@@ -376,6 +449,8 @@
         send_block(3, pair_side, z_send).wait_send()
         send_block(0, cross_side, cross_send).wait_send()
         send_block(1, cross_side, cross_send).wait_send()
+        send_across(0, cross_side, across_send.at[1]).wait_send()
+        send_across(2, pair_side, across_send.at[2]).wait_send()
 
     @pl.loop(0, chips)
     def _(chip):
@@ -402,9 +477,11 @@
     attention = pl.pallas_call(
         fused_kernel,
         out_shape=jax.ShapeDtypeStruct(queries.shape, jnp.bfloat16),
-        in_specs=[anywhere, anywhere, inside, inside],
+        in_specs=[anywhere, anywhere, inside, anywhere],
         out_specs=inside,
         scratch_shapes=[
+            pltpu.VMEM((1, count), jnp.int32),
+            pltpu.VMEM((queries.shape[1] // head_dim, count, count), jnp.float32),
             pltpu.VMEM((chips, 2 * count, depth), jnp.bfloat16),
             pltpu.VMEM((chips, depth, width), jnp.bfloat16),
             pltpu.VMEM(queries.shape, jnp.bfloat16),
@@ -414,13 +491,13 @@
             pltpu.VMEM((3 * count, width), jnp.bfloat16),
             pltpu.VMEM((count, head_dim), jnp.float32),
             pltpu.VMEM((count, head_dim), jnp.float32),
-            dma((chips,)), dma((chips,)), dma((chips,)), dma,
+            dma((chips,)), dma((chips,)), dma((chips,)), dma, dma,
             dma((chips,)), dma((2, chips)),
-            dma((4,)), dma((4,)), dma((4,)), dma((4,)), dma((4,)), dma((4,)),
+            dma((4,)), dma((4,)), dma((4,)), dma((4,)), dma((4,)), dma((4,)), dma((3,)),
             dma((2,)), dma((2,)), dma((2,)),
         ],
         compiler_params=pltpu.CompilerParams(
-            collective_id=0, has_side_effects=True, vmem_limit_bytes=40 * 1024 * 1024
+            collective_id=0, has_side_effects=True, vmem_limit_bytes=63 * 1024 * 1024
         ),
     )(tokens, queries, weight, positions.reshape(1, -1))
     return (attention, new_master, new_first, new_second)

time: 44 us -> 44.3 us (level); the launches traced: 43.4 us -> 44.1 us
  Pallas kernels: 36.8 us -> 38.9 us
  local copies, waits for them, and re-layouts: 2.96 us -> 1.67 us
    pallas_call x1, Pallas kernels: 36.8 us -> 38.9 us  [fused_local(): pl.pallas_call(fused_kernel, out_shape=jax.ShapeDtypeStruct(queries.shape...]
    unnamed x7 -> x1, local copies, waits for them, and re-layouts: 2.96 us -> 1.67 us
where the time goes in v2:
time: 44.3 us; the launch traced here: 44.1 us
  Pallas kernels  38.9 us (88%)
  other arithmetic  2.19 us (5%)
  local copies, waits for them, and re-layouts  1.67 us (4%)
  between operations  1.37 us (3%)
    pallas_call x1, Pallas kernels, fused_local(): pl.pallas_call(fused_kernel, out_shape=jax.ShapeDtypeStruct(queries.shape...  38.9 us
    convert_element_type x1, other arithmetic, fused_local(): weight = new_master.astype(jnp.bfloat16)  2.19 us
    unnamed x1, local copies, waits for them, and re-layouts  1.67 us

profile of v2, /device:TPU:9, one launch (start us, length us, event | category | flops | bytes accessed | tf_op | source)
XLA Modules:
  0.0 44.1 jit_solution(11194884136156745079)
XLA Ops:
  1.4 2.2 %fusion.1 = (bf16[256,256]{1,0:T(8,128)(2,1)}, f32[256,256]{1,0:T(8,128)}, f32[256,256]{1,0:T(8,128)}, f32[256,256]{1,0:T(8,128)}) fusion(f32[256,256]{1,0:T(8,128)} %param.12, f32[]{:T(128)} %bitcast.1, f32[]{:T(128)} %bitcast, f32[256,256]{1,0:T(8,128)} %param.11, f32[256,256]{1,0:T(8,128)} %param.13, f32[256,256]{1,0:T(8,128)} %param.14), kind=kLoop, calls=%fused_computation.4 | loop fusion | flops 917504 | bytes 1966088 | tf_op jit(solution)/shard_map/convert_element_type | solution.py:469
  3.6 38.9 %shard_map.111 = bf16[128,1024]{1,0:T(8,128)(2,1)} custom-call(bf16[128,8192]{1,0:T(8,128)(2,1)} %tok_hbm.1, bf16[128,1024]{1,0:T(8,128)(2,1)} %query_hbm.1, bf16[256,256]{1,0:T(8,128)(2,1)} %get-tuple-element.4.weight_ref, s32[1,128]{1,0:T(1,128)} %bitcast.3), custom_call_target="tpu_custom_call" | custom-call | tf_op jit(solution)/shard_map/pallas_call | solution.py:477
  42.4 1.7 %copy.14 = bf16[128,1024]{1,0:T(8,128)(2,1)} copy(bf16[128,1024]{1,0:T(8,128)(2,1)} %shard_map.111) | data formatting | bytes 524288

commit v3 on v2

--- a/solution.py
+++ b/solution.py
@@ -135,8 +135,8 @@
 
 def fused_kernel(
     tok_hbm, query_hbm, weight_ref, places_hbm, out_ref,
-    places_ref, own_scores, tok, blocks, query, rotated, part, back, kv, cosine, sine,
-    tok_sem, tok_send, tok_recv, query_sem, places_sem, block_recv, half_recv,
+    places_ref, own_scores, probs, tok, blocks, query, rotated, part, back, past_keys, past_values, cosine, sine,
+    tok_sem, tok_send, tok_recv, query_sem, places_sem, piece_recv,
     x_send, y_send, z_send, cross_send, half_x_send, half_y_send, across_send,
     back_sems, kv_send, kv_recv,
 ):
@@ -206,58 +206,70 @@
     def chip_at(plane, y_at, x_at):
         return plane * 4 + y_at * 2 + x_at
 
-    def send_block(step, device, sem):
-        chip = chip_at(order[step], y, x)
+    spots = {"line": (y, x), "along_x": (y, 1 - x), "along_y": (1 - y, x), "corner": (1 - y, 1 - x)}
+
+    def chip_of(kind, step):
+        return chip_at(order[step], *spots[kind])
+
+    def send_piece(kind, step, which, device, sem):
+        chip = chip_of(kind, step)
+        rows = pl.ds(which * half, half)
+        own_block = kind == "line" and step == 0
         return pltpu.make_async_remote_copy(
-            src_ref=weight_ref if step == 0 else blocks.at[chip],
-            dst_ref=blocks.at[chip],
-            send_sem=sem.at[step],
-            recv_sem=block_recv.at[chip],
+            src_ref=weight_ref.at[rows] if own_block else blocks.at[chip, rows],
+            dst_ref=blocks.at[chip, rows],
+            send_sem=sem,
+            recv_sem=piece_recv.at[which, chip],
             device_id=device,
             device_id_type=MESH,
         )
 
+    def send_line(step, which, side):
+        device, sem = {
+            "x": (x_side, x_send),
+            "y": (y_side, y_send),
+            "pair": (pair_side, z_send),
+            "cross": (cross_side, cross_send),
+        }[side]
+        return send_piece("line", step, which, device, sem.at[2 * step + which])
+
     def send_half(step, which):
-        chip = chip_at(order[step], y, 1 - x) if which == 0 else chip_at(order[step], 1 - y, x)
-        return pltpu.make_async_remote_copy(
-            src_ref=blocks.at[chip, pl.ds(which * half, half)],
-            dst_ref=blocks.at[chip, pl.ds(which * half, half)],
-            send_sem=(half_y_send if which == 0 else half_x_send).at[step],
-            recv_sem=half_recv.at[which, chip],
-            device_id=y_side if which == 0 else x_side,
-            device_id_type=MESH,
-        )
-
-    def send_across(step, device, sem):
-        chip = chip_at(order[step], 1 - y, 1 - x)
-        return pltpu.make_async_remote_copy(
-            src_ref=blocks.at[chip],
-            dst_ref=blocks.at[chip],
-            send_sem=sem,
-            recv_sem=block_recv.at[chip],
-            device_id=device,
-            device_id_type=MESH,
-        )
-
-    def block_arrival(chip):
-        pltpu.make_async_copy(blocks.at[chip], blocks.at[chip], block_recv.at[chip]).wait()
-
-    def half_arrival(which, chip):
-        place = blocks.at[chip, pl.ds(which * half, half)]
-        pltpu.make_async_copy(place, place, half_recv.at[which, chip]).wait()
+        if which == 0:
+            return send_piece("along_x", step, 0, y_side, half_y_send.at[step])
+        return send_piece("along_y", step, 1, x_side, half_x_send.at[step])
+
+    def send_corner(which, side):
+        device, offset = {"pair": (pair_side, 0), "cross": (cross_side, 2)}[side]
+        return send_piece("corner", 0, which, device, across_send.at[offset + which])
+
+    arrived = set()
+
+    def arrive(kind, step, which):
+        if (kind, step, which) not in arrived:
+            arrived.add((kind, step, which))
+            chip = chip_of(kind, step)
+            place = blocks.at[chip, pl.ds(which * half, half)]
+            pltpu.make_async_copy(place, place, piece_recv.at[which, chip]).wait()
 
     def add_block(chip, source):
         local_tokens(chip).wait()
         sent_tokens(chip).wait_recv()
         part[...] += jnp.dot(tok[chip], source[...], preferred_element_type=jnp.float32)
 
+    def add(kind, step):
+        arrive(kind, step, 0)
+        arrive(kind, step, 1)
+        chip = chip_of(kind, step)
+        add_block(chip, blocks.at[chip])
+
     steps = len(order)
-    for device, sem in ((x_side, x_send), (y_side, y_send), (pair_side, z_send)):
-        send_block(0, device, sem).start()
-
-    @pl.when(inner)
-    def _():
-        send_block(0, cross_side, cross_send).start()
+    for which in range(2):
+        for side in ("x", "y", "pair"):
+            send_line(0, which, side).start()
+
+        @pl.when(inner)
+        def _():
+            send_line(0, which, "cross").start()
 
     @pl.loop(0, chips)
     def _(chip):
@@ -265,6 +277,44 @@
         local_tokens(chip).start()
 
     part[...] = jnp.zeros_like(part)
+
+    def rotate(values_in):
+        return values_in * cosine[...] + pltpu.roll(values_in, head_dim // 2, 1) * sine[...]
+
+    def forward_half(step, which):
+        arrive("along_y" if which else "along_x", step, which)
+        send_half(step, which).start()
+
+    def forward_line(step, which):
+        arrive("line", step, which)
+
+        @pl.when(inner)
+        def _():
+            send_line(step, which, "cross" if step == 1 else "pair").start()
+
+        send_line(step, which, "x").start()
+        send_line(step, which, "y").start()
+
+    forward_half(0, 0)
+    forward_line(1, 0)
+    forward_half(0, 1)
+    forward_line(1, 1)
+    add_block(chip_of("line", 0), weight_ref)
+    forward_line(2, 0)
+    forward_line(2, 1)
+    for which in range(2):
+        arrive("corner", 0, which)
+        send_corner(which, "pair").start()
+
+        @pl.when(inner)
+        def _():
+            send_corner(which, "cross").start()
+
+    add("line", 1)
+    add("along_x", 0)
+    add("along_y", 0)
+    forward_line(3, 0)
+    forward_line(3, 1)
 
     places_copy.wait()
     row = lax.broadcasted_iota(jnp.int32, (count, count), 0)
@@ -273,119 +323,85 @@
         jnp.where(row == lane, places_ref[...].astype(jnp.float32), 0.0), axis=1, keepdims=True
     )
     cosine[...], sine[...] = rope_tables(places, head_dim)
-
-    def rotate(values_in):
-        return values_in * cosine[...] + pltpu.roll(values_in, head_dim // 2, 1) * sine[...]
-
-    own_chip = chip_at(z, y, x)
-    line = [chip_at(plane, y, x) for plane in order]
-    along_x = [chip_at(plane, y, 1 - x) for plane in order]
-    along_y = [chip_at(plane, 1 - y, x) for plane in order]
-    corner = [chip_at(plane, 1 - y, 1 - x) for plane in order]
-
-    def add_blocks(*chips_in):
-        for chip in chips_in:
-            add_block(chip, blocks.at[chip])
-
-    def forward_halves(step):
-        for which, chip in enumerate((along_x[step], along_y[step])):
-            block_arrival(chip)
-            send_half(step, which).start()
-
-    def forward_line(step):
-        block_arrival(line[step])
-
-        @pl.when(inner)
+    add("corner", 0)
+    add("line", 2)
+    add("along_x", 1)
+    add("along_y", 1)
+    outer = (z == 0) | (z == 3)
+    for which in range(2):
+        arrive("along_y" if which else "along_x", 2, which)
+
+        @pl.when(outer)
         def _():
-            if step == 1:
-                send_block(step, cross_side, cross_send).start()
-            else:
-                send_block(step, pair_side, z_send).start()
-
-        send_block(step, x_side, x_send).start()
-        send_block(step, y_side, y_send).start()
+            send_half(2, which).start()
 
     query_copy.wait()
     heads = query.shape[1] // head_dim
-    add_block(own_chip, weight_ref)
-    forward_halves(0)
-    forward_line(1)
-    forward_line(2)
-    half_arrival(0, corner[0])
-    half_arrival(1, corner[0])
-    send_across(0, pair_side, across_send.at[0]).start()
-
-    @pl.when(inner)
-    def _():
-        send_across(0, cross_side, across_send.at[1]).start()
-
     for head in range(heads):
         at = slice(head * head_dim, (head + 1) * head_dim)
         rotated[:, at] = rotate(query[:, at].astype(jnp.float32)).astype(jnp.bfloat16)
-    forward_line(3)
-    add_blocks(along_x[0], along_y[0], line[1])
-
-    @pl.when(inner)
-    def _():
-        block_arrival(corner[2])
-        send_across(2, pair_side, across_send.at[2]).start()
-
-    add_blocks(line[2], corner[0])
-    block_arrival(along_x[1])
-    block_arrival(along_y[1])
-    add_blocks(along_x[1], along_y[1])
-    block_arrival(along_x[2])
-    block_arrival(along_y[2])
-    forward_halves(3)
-    add_blocks(along_x[2], along_y[2], line[3], along_x[3], along_y[3])
-    block_arrival(corner[1])
-    add_blocks(corner[1])
-
-    @pl.when((z == 0) | (z == 3))
-    def _():
-        block_arrival(corner[2])
-
-    add_blocks(corner[2])
-    half_arrival(0, corner[3])
-    half_arrival(1, corner[3])
-    add_blocks(corner[3])
-
-    back_copy = pltpu.make_async_remote_copy(
-        src_ref=part.at[rows_of(1 - core)],
-        dst_ref=back,
-        send_sem=back_sems.at[0],
-        recv_sem=back_sems.at[1],
-        device_id=peer,
-        device_id_type=MESH,
-    )
-    back_copy.start()
-    back_copy.wait_recv()
-    projected = part[rows_of(core)] + back[...]
+    add("line", 3)
+    forward_half(3, 0)
+    forward_half(3, 1)
+    add("along_x", 2)
+    add("along_y", 2)
+    add("corner", 1)
+    add("along_x", 3)
+    add("along_y", 3)
+    add("corner", 2)
+    add("corner", 3)
+
+    sides = (pl.ds(0, head_dim), pl.ds(head_dim, head_dim))
+
+    def back_copy(side):
+        return pltpu.make_async_remote_copy(
+            src_ref=part.at[rows_of(1 - core), sides[side]],
+            dst_ref=back.at[:, sides[side]],
+            send_sem=back_sems.at[0, side],
+            recv_sem=back_sems.at[1, side],
+            device_id=peer,
+            device_id_type=MESH,
+        )
+
     own = pl.ds(2 * count, count)
-    kv[own, :head_dim] = rotate(projected[:, :head_dim]).astype(jnp.bfloat16)
-    kv[own, head_dim:] = projected[:, head_dim:].astype(jnp.bfloat16)
-
-    def send_kv(distance):
+    pasts = (past_keys, past_values)
+
+    def send_past(side, distance):
         return pltpu.make_async_remote_copy(
-            src_ref=kv.at[own],
-            dst_ref=kv.at[pl.ds((2 - distance) * count, count)],
-            send_sem=kv_send.at[distance - 1],
-            recv_sem=kv_recv.at[distance - 1],
+            src_ref=pasts[side].at[own],
+            dst_ref=pasts[side].at[pl.ds((2 - distance) * count, count)],
+            send_sem=kv_send.at[side, distance - 1],
+            recv_sem=kv_recv.at[side, distance - 1],
             device_id=ordinal(next_one if distance == 1 else next_two),
             device_id_type=MESH,
         )
 
-    for distance in (1, 2):
-
-        @pl.when(me < total - distance)
-        def _():
-            send_kv(distance).start()
-
-        @pl.when(me < distance)
-        def _():
-            kv[pl.ds((2 - distance) * count, count), :] = jnp.zeros(
-                (count, 2 * head_dim), jnp.bfloat16
-            )
+    back_copy(0).start()
+    back_copy(1).start()
+    for side in range(2):
+        back_copy(side).wait_recv()
+        projected = part[rows_of(core), sides[side]] + back[:, sides[side]]
+        if side == 0:
+            projected = rotate(projected)
+        pasts[side][own, :] = projected.astype(jnp.bfloat16)
+        for distance in (2, 1):
+
+            @pl.when(me < total - distance)
+            def _():
+                send_past(side, distance).start()
+
+            @pl.when(me < distance)
+            def _():
+                pasts[side][pl.ds((2 - distance) * count, count), :] = jnp.zeros(
+                    (count, head_dim), jnp.bfloat16
+                )
+
+    def past_arrival(side):
+        for distance in (1, 2):
+
+            @pl.when(me >= distance)
+            def _():
+                send_past(side, distance).wait_recv()
 
     near_limit = row - places.astype(jnp.int32)
     early = lax.broadcasted_iota(jnp.int32, (count, 2 * count), 1) - 2 * count
@@ -401,22 +417,14 @@
         ) * head_dim ** (-0.5)
         return jnp.where(allowed, scores, masked_score)
 
-    own_keys = kv[own, :head_dim]
+    own_keys = past_keys[own, :]
     for head in range(heads):
         own_scores[head] = score(head, own_keys, allowed_own)
 
-    for distance in (1, 2):
-
-        @pl.when(me >= distance)
-        def _():
-            send_kv(distance).wait_recv()
-
     past = pl.ds(0, 2 * count)
-    early_keys = kv[past, :head_dim]
-    early_values = kv[past, head_dim:]
-    own_values = kv[own, head_dim:]
+    past_arrival(0)
+    early_keys = past_keys[past, :]
     for head in range(heads):
-        at = slice(head * head_dim, (head + 1) * head_dim)
         near = own_scores[head]
         far = score(head, early_keys, allowed_early)
         top = jnp.maximum(
@@ -427,41 +435,47 @@
         share = 1.0 / (
             jnp.sum(near, axis=1, keepdims=True) + jnp.sum(far, axis=1, keepdims=True)
         )
-        result = jnp.dot(
-            (near * share).astype(jnp.bfloat16), own_values, preferred_element_type=jnp.float32
-        ) + jnp.dot(
-            (far * share).astype(jnp.bfloat16), early_values, preferred_element_type=jnp.float32
-        )
-        out_ref[:, at] = result.astype(jnp.bfloat16)
-
-    for step in range(steps):
-        send_block(step, x_side, x_send).wait_send()
-        send_block(step, y_side, y_send).wait_send()
-    for step in (0, 3):
-        send_half(step, 0).wait_send()
-        send_half(step, 1).wait_send()
-    send_block(0, pair_side, z_send).wait_send()
-    send_across(0, pair_side, across_send.at[0]).wait_send()
-
-    @pl.when(inner)
-    def _():
-        send_block(2, pair_side, z_send).wait_send()
-        send_block(3, pair_side, z_send).wait_send()
-        send_block(0, cross_side, cross_send).wait_send()
-        send_block(1, cross_side, cross_send).wait_send()
-        send_across(0, cross_side, across_send.at[1]).wait_send()
-        send_across(2, pair_side, across_send.at[2]).wait_send()
+        probs[head, :, : 2 * count] = (far * share).astype(jnp.bfloat16)
+        probs[head, :, 2 * count :] = (near * share).astype(jnp.bfloat16)
+    past_arrival(1)
+    values_v = past_values[...]
+    for head in range(heads):
+        out_ref[:, head * head_dim : (head + 1) * head_dim] = jnp.dot(
+            probs[head], values_v, preferred_element_type=jnp.float32
+        ).astype(jnp.bfloat16)
+
+    for which in range(2):
+        for step in range(steps):
+            send_line(step, which, "x").wait_send()
+            send_line(step, which, "y").wait_send()
+        send_half(0, which).wait_send()
+        send_half(3, which).wait_send()
+        send_line(0, which, "pair").wait_send()
+        send_corner(which, "pair").wait_send()
+
+        @pl.when(outer)
+        def _():
+            send_half(2, which).wait_send()
+
+        @pl.when(inner)
+        def _():
+            send_line(2, which, "pair").wait_send()
+            send_line(3, which, "pair").wait_send()
+            send_line(0, which, "cross").wait_send()
+            send_line(1, which, "cross").wait_send()
+            send_corner(which, "cross").wait_send()
 
     @pl.loop(0, chips)
     def _(chip):
         sent_tokens(chip).wait_send()
 
-    back_copy.wait_send()
-    for distance in (1, 2):
-
-        @pl.when(me < total - distance)
-        def _():
-            send_kv(distance).wait_send()
+    for side in range(2):
+        back_copy(side).wait_send()
+        for distance in (1, 2):
+
+            @pl.when(me < total - distance)
+            def _():
+                send_past(side, distance).wait_send()
 
 
 def fused_local(tokens, queries, positions, grad, master, moment1, moment2, step):
@@ -482,22 +496,24 @@
         scratch_shapes=[
             pltpu.VMEM((1, count), jnp.int32),
             pltpu.VMEM((queries.shape[1] // head_dim, count, count), jnp.float32),
+            pltpu.VMEM((queries.shape[1] // head_dim, count, 3 * count), jnp.bfloat16),
             pltpu.VMEM((chips, 2 * count, depth), jnp.bfloat16),
             pltpu.VMEM((chips, depth, width), jnp.bfloat16),
             pltpu.VMEM(queries.shape, jnp.bfloat16),
             pltpu.VMEM(queries.shape, jnp.bfloat16),
             pltpu.VMEM((2 * count, width), jnp.float32),
             pltpu.VMEM((count, width), jnp.float32),
-            pltpu.VMEM((3 * count, width), jnp.bfloat16),
+            pltpu.VMEM((3 * count, head_dim), jnp.bfloat16),
+            pltpu.VMEM((3 * count, head_dim), jnp.bfloat16),
             pltpu.VMEM((count, head_dim), jnp.float32),
             pltpu.VMEM((count, head_dim), jnp.float32),
             dma((chips,)), dma((chips,)), dma((chips,)), dma, dma,
-            dma((chips,)), dma((2, chips)),
-            dma((4,)), dma((4,)), dma((4,)), dma((4,)), dma((4,)), dma((4,)), dma((3,)),
-            dma((2,)), dma((2,)), dma((2,)),
+            dma((2, chips)),
+            dma((8,)), dma((8,)), dma((8,)), dma((4,)), dma((4,)), dma((4,)), dma((4,)),
+            dma((2, 2)), dma((2, 2)), dma((2, 2)),
         ],
         compiler_params=pltpu.CompilerParams(
-            collective_id=0, has_side_effects=True, vmem_limit_bytes=63 * 1024 * 1024
+            collective_id=0, has_side_effects=True, vmem_limit_bytes=62 * 1024 * 1024
         ),
     )(tokens, queries, weight, positions.reshape(1, -1))
     return (attention, new_master, new_first, new_second)

time: 44.3 us -> 40.6 us (0.916)
  Pallas kernels: 38.9 us -> 34.9 us
    pallas_call x1, Pallas kernels: 38.9 us -> 34.9 us  [fused_local(): pl.pallas_call(fused_kernel, out_shape=jax.ShapeDtypeStruct(queries.shape...]
where the time goes in v3:
time: 40.6 us; the launch traced here: 40.1 us
  Pallas kernels  34.9 us (86%)
  other arithmetic  2.19 us (5%)
  local copies, waits for them, and re-layouts  1.67 us (4%)
  between operations  1.37 us (3%)
    pallas_call x1, Pallas kernels, fused_local(): pl.pallas_call(fused_kernel, out_shape=jax.ShapeDtypeStruct(queries.shape...  34.9 us
    convert_element_type x1, other arithmetic, fused_local(): weight = new_master.astype(jnp.bfloat16)  2.19 us
    unnamed x1, local copies, waits for them, and re-layouts  1.67 us

profile of v3, /device:TPU:9, one launch (start us, length us, event | category | flops | bytes accessed | tf_op | source)
XLA Modules:
  0.0 40.1 jit_solution(577810679265935410)
XLA Ops:
  1.4 2.2 %fusion.1 = (bf16[256,256]{1,0:T(8,128)(2,1)}, f32[256,256]{1,0:T(8,128)}, f32[256,256]{1,0:T(8,128)}, f32[256,256]{1,0:T(8,128)}) fusion(f32[256,256]{1,0:T(8,128)} %param.12, f32[]{:T(128)} %bitcast.1, f32[]{:T(128)} %bitcast, f32[256,256]{1,0:T(8,128)} %param.11, f32[256,256]{1,0:T(8,128)} %param.13, f32[256,256]{1,0:T(8,128)} %param.14), kind=kLoop, calls=%fused_computation.4 | loop fusion | flops 917504 | bytes 1966088 | tf_op jit(solution)/shard_map/convert_element_type | solution.py:483
  3.6 34.9 %shard_map.111 = bf16[128,1024]{1,0:T(8,128)(2,1)} custom-call(bf16[128,8192]{1,0:T(8,128)(2,1)} %tok_hbm.1, bf16[128,1024]{1,0:T(8,128)(2,1)} %query_hbm.1, bf16[256,256]{1,0:T(8,128)(2,1)} %get-tuple-element.4.weight_ref, s32[1,128]{1,0:T(1,128)} %bitcast.3), custom_call_target="tpu_custom_call" | custom-call | tf_op jit(solution)/shard_map/pallas_call | solution.py:491
  38.5 1.7 %copy.14 = bf16[128,1024]{1,0:T(8,128)(2,1)} copy(bf16[128,1024]{1,0:T(8,128)(2,1)} %shard_map.111) | data formatting | bytes 524288

commit v4 on v3

--- a/solution.py
+++ b/solution.py
@@ -135,7 +135,7 @@
 
 def fused_kernel(
     tok_hbm, query_hbm, weight_ref, places_hbm, out_ref,
-    places_ref, own_scores, probs, tok, blocks, query, rotated, part, back, past_keys, past_values, cosine, sine,
+    places_ref, own_scores, probs, tok, blocks, query, rotated, part, back, past_keys, past_values, places, cosine, sine,
     tok_sem, tok_send, tok_recv, query_sem, places_sem, piece_recv,
     x_send, y_send, z_send, cross_send, half_x_send, half_y_send, across_send,
     back_sems, kv_send, kv_recv,
@@ -285,71 +285,88 @@
         arrive("along_y" if which else "along_x", step, which)
         send_half(step, which).start()
 
-    def forward_line(step, which):
+    def forward_line(step, which, onward=None):
         arrive("line", step, which)
-
-        @pl.when(inner)
-        def _():
-            send_line(step, which, "cross" if step == 1 else "pair").start()
-
+        if onward is not None:
+            send_line(step, which, onward).start()
         send_line(step, which, "x").start()
         send_line(step, which, "y").start()
 
-    forward_half(0, 0)
-    forward_line(1, 0)
-    forward_half(0, 1)
-    forward_line(1, 1)
-    add_block(chip_of("line", 0), weight_ref)
-    forward_line(2, 0)
-    forward_line(2, 1)
-    for which in range(2):
-        arrive("corner", 0, which)
-        send_corner(which, "pair").start()
-
-        @pl.when(inner)
-        def _():
-            send_corner(which, "cross").start()
-
-    add("line", 1)
-    add("along_x", 0)
-    add("along_y", 0)
-    forward_line(3, 0)
-    forward_line(3, 1)
-
-    places_copy.wait()
     row = lax.broadcasted_iota(jnp.int32, (count, count), 0)
     lane = lax.broadcasted_iota(jnp.int32, (count, count), 1)
-    places = jnp.sum(
-        jnp.where(row == lane, places_ref[...].astype(jnp.float32), 0.0), axis=1, keepdims=True
-    )
-    cosine[...], sine[...] = rope_tables(places, head_dim)
-    add("corner", 0)
-    add("line", 2)
-    add("along_x", 1)
-    add("along_y", 1)
+    heads = query.shape[1] // head_dim
+
+    def prepare():
+        places_copy.wait()
+        places[...] = jnp.sum(
+            jnp.where(row == lane, places_ref[...].astype(jnp.float32), 0.0),
+            axis=1,
+            keepdims=True,
+        )
+        cosine[...], sine[...] = rope_tables(places[...], head_dim)
+        query_copy.wait()
+        for head in range(heads):
+            at = slice(head * head_dim, (head + 1) * head_dim)
+            rotated[:, at] = rotate(query[:, at].astype(jnp.float32)).astype(jnp.bfloat16)
+
     outer = (z == 0) | (z == 3)
-    for which in range(2):
-        arrive("along_y" if which else "along_x", 2, which)
-
-        @pl.when(outer)
-        def _():
-            send_half(2, which).start()
-
-    query_copy.wait()
-    heads = query.shape[1] // head_dim
-    for head in range(heads):
-        at = slice(head * head_dim, (head + 1) * head_dim)
-        rotated[:, at] = rotate(query[:, at].astype(jnp.float32)).astype(jnp.bfloat16)
-    add("line", 3)
-    forward_half(3, 0)
-    forward_half(3, 1)
-    add("along_x", 2)
-    add("along_y", 2)
-    add("corner", 1)
-    add("along_x", 3)
-    add("along_y", 3)
-    add("corner", 2)
-    add("corner", 3)
+
+    @pl.when(inner)
+    def _():
+        arrived.clear()
+        for which in range(2):
+            forward_half(0, which)
+            forward_line(1, which, "cross")
+            forward_line(2, which, "pair")
+        add_block(chip_of("line", 0), weight_ref)
+        for which in range(2):
+            arrive("corner", 0, which)
+            send_corner(which, "cross").start()
+        for which in range(2):
+            forward_line(3, which, "pair")
+        for which in range(2):
+            send_corner(which, "pair").start()
+        for item in (("along_x", 0), ("along_y", 0), ("line", 1), ("line", 2), ("corner", 0)):
+            add(*item)
+        prepare()
+        for item in (("along_x", 1), ("along_y", 1), ("along_x", 2), ("along_y", 2)):
+            add(*item)
+        forward_half(3, 0)
+        forward_half(3, 1)
+        for item in (("line", 3), ("corner", 1), ("along_x", 3), ("along_y", 3)):
+            add(*item)
+        add("corner", 2)
+        add("corner", 3)
+
+    @pl.when(outer)
+    def _():
+        arrived.clear()
+        for which in range(2):
+            forward_half(0, which)
+            forward_line(1, which)
+        add_block(chip_of("line", 0), weight_ref)
+        for which in range(2):
+            arrive("corner", 0, which)
+            send_corner(which, "pair").start()
+        forward_line(2, 0)
+        forward_line(2, 1)
+        for item in (("along_x", 0), ("along_y", 0), ("line", 1), ("corner", 0)):
+            add(*item)
+        forward_line(3, 0)
+        forward_line(3, 1)
+        prepare()
+        for item in (("along_x", 1), ("along_y", 1), ("line", 2)):
+            add(*item)
+        forward_half(2, 0)
+        forward_half(2, 1)
+        add("along_x", 2)
+        add("along_y", 2)
+        forward_half(3, 0)
+        forward_half(3, 1)
+        for item in (("line", 3), ("corner", 1), ("along_x", 3), ("along_y", 3)):
+            add(*item)
+        add("corner", 2)
+        add("corner", 3)
 
     sides = (pl.ds(0, head_dim), pl.ds(head_dim, head_dim))
 
@@ -403,7 +420,7 @@
             def _():
                 send_past(side, distance).wait_recv()
 
-    near_limit = row - places.astype(jnp.int32)
+    near_limit = row - places[...].astype(jnp.int32)
     early = lax.broadcasted_iota(jnp.int32, (count, 2 * count), 1) - 2 * count
     allowed_own = (lane <= row) & (lane >= near_limit)
     allowed_early = early >= near_limit[:, :1]
@@ -505,6 +522,7 @@
             pltpu.VMEM((count, width), jnp.float32),
             pltpu.VMEM((3 * count, head_dim), jnp.bfloat16),
             pltpu.VMEM((3 * count, head_dim), jnp.bfloat16),
+            pltpu.VMEM((count, 1), jnp.float32),
             pltpu.VMEM((count, head_dim), jnp.float32),
             pltpu.VMEM((count, head_dim), jnp.float32),
             dma((chips,)), dma((chips,)), dma((chips,)), dma, dma,
@@ -513,7 +531,7 @@
             dma((2, 2)), dma((2, 2)), dma((2, 2)),
         ],
         compiler_params=pltpu.CompilerParams(
-            collective_id=0, has_side_effects=True, vmem_limit_bytes=62 * 1024 * 1024
+            collective_id=0, has_side_effects=True, vmem_limit_bytes=121 * 512 * 1024
         ),
     )(tokens, queries, weight, positions.reshape(1, -1))
     return (attention, new_master, new_first, new_second)

time: 40.6 us -> 39.5 us (0.973)
  Pallas kernels: 34.9 us -> 33.6 us
    pallas_call x1, Pallas kernels: 34.9 us -> 33.6 us  [fused_local(): pl.pallas_call(fused_kernel, out_shape=jax.ShapeDtypeStruct(queries.shape...]
where the time goes in v4:
time: 39.5 us; the launch traced here: 38.8 us
  Pallas kernels  33.6 us (85%)
  other arithmetic  2.19 us (6%)
  local copies, waits for them, and re-layouts  1.67 us (4%)
  between operations  1.37 us (3%)
    pallas_call x1, Pallas kernels, fused_local(): pl.pallas_call(fused_kernel, out_shape=jax.ShapeDtypeStruct(queries.shape...  33.6 us
    convert_element_type x1, other arithmetic, fused_local(): weight = new_master.astype(jnp.bfloat16)  2.19 us
    unnamed x1, local copies, waits for them, and re-layouts  1.67 us

profile of v4, /device:TPU:9, one launch (start us, length us, event | category | flops | bytes accessed | tf_op | source)
XLA Modules:
  0.0 38.8 jit_solution(10978794339306612214)
XLA Ops:
  1.4 2.2 %fusion.1 = (bf16[256,256]{1,0:T(8,128)(2,1)}, f32[256,256]{1,0:T(8,128)}, f32[256,256]{1,0:T(8,128)}, f32[256,256]{1,0:T(8,128)}) fusion(f32[256,256]{1,0:T(8,128)} %param.12, f32[]{:T(128)} %bitcast.1, f32[]{:T(128)} %bitcast, f32[256,256]{1,0:T(8,128)} %param.11, f32[256,256]{1,0:T(8,128)} %param.13, f32[256,256]{1,0:T(8,128)} %param.14), kind=kLoop, calls=%fused_computation.4 | loop fusion | flops 917504 | bytes 1966088 | tf_op jit(solution)/shard_map/convert_element_type | solution.py:500
  3.6 33.6 %shard_map.111 = bf16[128,1024]{1,0:T(8,128)(2,1)} custom-call(bf16[128,8192]{1,0:T(8,128)(2,1)} %tok_hbm.1, bf16[128,1024]{1,0:T(8,128)(2,1)} %query_hbm.1, bf16[256,256]{1,0:T(8,128)(2,1)} %get-tuple-element.4.weight_ref, s32[1,128]{1,0:T(1,128)} %bitcast.3), custom_call_target="tpu_custom_call" | custom-call | tf_op jit(solution)/shard_map/pallas_call | solution.py:508
  37.2 1.7 %copy.14 = bf16[128,1024]{1,0:T(8,128)(2,1)} copy(bf16[128,1024]{1,0:T(8,128)(2,1)} %shard_map.111) | data formatting | bytes 524288

commit v5 on v4

--- a/solution.py
+++ b/solution.py
@@ -136,7 +136,7 @@
 def fused_kernel(
     tok_hbm, query_hbm, weight_ref, places_hbm, out_ref,
     places_ref, own_scores, probs, tok, blocks, query, rotated, part, back, past_keys, past_values, places, cosine, sine,
-    tok_sem, tok_send, tok_recv, query_sem, places_sem, piece_recv,
+    tok_sem, tok_send, tok_recv, query_sem, places_sem, weight_sem, piece_recv,
     x_send, y_send, z_send, cross_send, half_x_send, half_y_send, across_send,
     back_sems, kv_send, kv_recv,
 ):
@@ -271,6 +271,10 @@
         def _():
             send_line(0, which, "cross").start()
 
+    own_place = blocks.at[chip_of("line", 0)]
+    weight_copy = pltpu.make_async_copy(weight_ref, own_place, weight_sem)
+    weight_copy.start()
+
     @pl.loop(0, chips)
     def _(chip):
         sent_tokens(chip).start()
@@ -318,7 +322,8 @@
             forward_half(0, which)
             forward_line(1, which, "cross")
             forward_line(2, which, "pair")
-        add_block(chip_of("line", 0), weight_ref)
+        weight_copy.wait()
+        add_block(chip_of("line", 0), own_place)
         for which in range(2):
             arrive("corner", 0, which)
             send_corner(which, "cross").start()
@@ -344,7 +349,8 @@
         for which in range(2):
             forward_half(0, which)
             forward_line(1, which)
-        add_block(chip_of("line", 0), weight_ref)
+        weight_copy.wait()
+        add_block(chip_of("line", 0), own_place)
         for which in range(2):
             arrive("corner", 0, which)
             send_corner(which, "pair").start()
@@ -507,8 +513,8 @@
     inside = pl.BlockSpec(memory_space=pltpu.VMEM)
     attention = pl.pallas_call(
         fused_kernel,
-        out_shape=jax.ShapeDtypeStruct(queries.shape, jnp.bfloat16),
-        in_specs=[anywhere, anywhere, inside, anywhere],
+        out_shape=pltpu.VMEM(queries.shape, jnp.bfloat16),
+        in_specs=[anywhere, anywhere, anywhere, anywhere],
         out_specs=inside,
         scratch_shapes=[
             pltpu.VMEM((1, count), jnp.int32),
@@ -525,7 +531,7 @@
             pltpu.VMEM((count, 1), jnp.float32),
             pltpu.VMEM((count, head_dim), jnp.float32),
             pltpu.VMEM((count, head_dim), jnp.float32),
-            dma((chips,)), dma((chips,)), dma((chips,)), dma, dma,
+            dma((chips,)), dma((chips,)), dma((chips,)), dma, dma, dma,
             dma((2, chips)),
             dma((8,)), dma((8,)), dma((8,)), dma((4,)), dma((4,)), dma((4,)), dma((4,)),
             dma((2, 2)), dma((2, 2)), dma((2, 2)),

time: 39.5 us -> 37.2 us (0.942)
  Pallas kernels: 33.6 us -> 32.3 us
  local copies, waits for them, and re-layouts: 1.67 us -> 0.71 us
    pallas_call x1, Pallas kernels: 33.6 us -> 32.3 us  [fused_local(): pl.pallas_call(fused_kernel, out_shape=pltpu.VMEM(queries.shape, jnp.bflo...]
    unnamed x1, local copies, waits for them, and re-layouts: 1.67 us -> 0.71 us
where the time goes in v5:
time: 37.2 us; the launch traced here: 36.6 us
  Pallas kernels  32.3 us (87%)
  other arithmetic  2.19 us (6%)
  between operations  1.37 us (4%)
  local copies, waits for them, and re-layouts  0.71 us (2%)
    pallas_call x1, Pallas kernels, fused_local(): pl.pallas_call(fused_kernel, out_shape=pltpu.VMEM(queries.shape, jnp.bflo...  32.3 us
    convert_element_type x1, other arithmetic, fused_local(): weight = new_master.astype(jnp.bfloat16)  2.19 us

profile of v5, /device:TPU:9, one launch (start us, length us, event | category | flops | bytes accessed | tf_op | source)
XLA Modules:
  0.0 36.6 jit_solution(8596296088722163239)
XLA Ops:
  1.4 2.2 %fusion.1 = (bf16[256,256]{1,0:T(8,128)(2,1)}, f32[256,256]{1,0:T(8,128)}, f32[256,256]{1,0:T(8,128)}, f32[256,256]{1,0:T(8,128)}) fusion(f32[256,256]{1,0:T(8,128)} %param.12, f32[]{:T(128)} %bitcast.1, f32[]{:T(128)} %bitcast, f32[256,256]{1,0:T(8,128)} %param.11, f32[256,256]{1,0:T(8,128)} %param.13, f32[256,256]{1,0:T(8,128)} %param.14), kind=kLoop, calls=%fused_computation.4 | loop fusion | flops 917504 | bytes 1966088 | tf_op jit(solution)/shard_map/convert_element_type | solution.py:506
  3.6 32.3 %shard_map.111 = bf16[128,1024]{1,0:T(8,128)(2,1)S(1)} custom-call(bf16[128,8192]{1,0:T(8,128)(2,1)} %tok_hbm.1, bf16[128,1024]{1,0:T(8,128)(2,1)} %query_hbm.1, bf16[256,256]{1,0:T(8,128)(2,1)} %get-tuple-element.4.weight_ref, s32[1,128]{1,0:T(1,128)} %bitcast.3), custom_call_target="tpu_custom_call" | custom-call | tf_op jit(solution)/shard_map/pallas_call | solution.py:514
  35.9 0.7 %copy.13 = bf16[128,1024]{1,0:T(8,128)(2,1)} copy(bf16[128,1024]{1,0:T(8,128)(2,1)S(1)} %shard_map.111) | data formatting | bytes 524288
